TPU v7x, 32 devices: a whole 2x2x4 slice. The times are simulated.
32 devices in a mesh: dp: 4 (over y, core), expert: 8 (over z, x).
Axes of the slice: x: 2, y: 2, z: 4, core: 2. Of those that a mesh axis runs over, the one named last changes fastest.
Arguments:
- out_grad: bfloat16 [4096, 7168], P(('dp', 'expert')), may hold values from -6 to 6
- gate_weights: bfloat16 [4096, 8], P(('dp', 'expert')), may hold values from 0.099609375 to 1
- routes: int32 [4096, 8], P(('dp', 'expert')), may hold values from 0 to 63, all different within a row; in each aligned block of 128 rows (0 to 127, 128 to 255, ...) at most 24 rows name the same one
- seq_ids: int32 [32, 128], P(('dp', 'expert')), may hold values from 0 to 1, never falling along the last dimension, each value on 1 to 96 neighbouring positions
- hidden: bfloat16 [32, 64, 24, 2048], P('dp', 'expert'), may hold values from -6 to 6
- proj_out: bfloat16 [7168, 128], P('expert'), may hold values from -0.0625 to 0.0625
- proj_in: bfloat16 [2048, 32], P('dp'), may hold values from -0.125 to 0.125
Outputs:
- seq_grads: bfloat16 [64, 64, 4096], P('dp', 'expert')
Inputs may be any that keep to these rules, and one draw needn't show every extreme that they name: `routes`: in the rows of one device (aligned blocks of 128 tokens) no expert is named by more than 24 rows, a bound that some block reaches; a token names 8 different experts. `seq_ids`: within each block never falling; every id of 0 to 1 occurs, no sequence has more than 96 tokens.
All inputs are finite; a program needn't handle non-finite values.
Results may differ from a plain program's by a relative error of at most 0.0085.
Values may be sent and summed in bfloat16 or wider, within the bound.
A program may use at most 128 MiB of HBM per device.

v0:
```python
import jax
import jax.numpy as jnp
from jax import lax
from jax.sharding import PartitionSpec as P

SEQ_DEV = 2


def slot_rows(route_block, gate_block, seq_block, grad_block, first_slot, slot_count, capacity):
    token_count = route_block.shape[0]
    choice_count = route_block.shape[1]
    pair_count = token_count * choice_count
    flat_routes = route_block.reshape(-1)
    order = jnp.arange(pair_count, dtype=jnp.int32)
    same = flat_routes[:, None] == flat_routes[None, :]
    before = order[None, :] < order[:, None]
    ranks = jnp.sum((same & before).astype(jnp.int32), axis=1)
    positions = (flat_routes * capacity + ranks).astype(jnp.int32)
    wanted = first_slot + jnp.arange(slot_count, dtype=jnp.int32)
    select = positions[None, :] == wanted[:, None]
    pair_gate = gate_block.reshape(-1).astype(jnp.float32)
    slot_gate = jnp.sum(jnp.where(select, pair_gate[None, :], 0.0), axis=1).astype(jnp.bfloat16)
    pair_seq = jnp.broadcast_to(seq_block[:, None], (token_count, choice_count)).reshape(-1)
    slot_seq = jnp.sum(jnp.where(select, pair_seq[None, :], 0), axis=1).astype(jnp.int32)
    token_pick = jnp.any(select.reshape(slot_count, token_count, choice_count), axis=2).astype(
        jnp.bfloat16
    )
    slot_grad = jnp.dot(token_pick, grad_block, preferred_element_type=jnp.float32).astype(
        jnp.bfloat16
    )
    return (slot_grad, slot_gate, slot_seq)


def sequence_totals(grad_slots, hidden_proj, slot_gate, slot_seq):
    weighted = (slot_seq[..., None] == jnp.arange(SEQ_DEV, dtype=jnp.int32)).astype(
        jnp.float32
    ) * slot_gate.astype(jnp.float32)[..., None]
    totals = jnp.einsum(
        "becs,beco,beci->bseoi",
        weighted,
        grad_slots.astype(jnp.float32),
        hidden_proj.astype(jnp.float32),
        precision=lax.Precision.HIGHEST,
    )
    groups, seq_count, local_count, k_out, k_in = totals.shape
    return totals.reshape(groups * seq_count, local_count, k_out * k_in).astype(jnp.bfloat16)


def shards(out_grad, gate_weights, routes, seq_ids, hidden, proj_out, proj_in):
    groups = lax.axis_size("expert")
    local_count = hidden.shape[1]
    capacity = hidden.shape[2]
    feature_width = hidden.shape[3]
    token_count = out_grad.shape[0]
    k_out = proj_out.shape[1]
    k_in = proj_in.shape[1]
    proj_full = lax.all_gather(proj_out, "expert", axis=0, tiled=True)
    grad_proj = jnp.dot(out_grad, proj_full, preferred_element_type=jnp.float32).astype(
        jnp.bfloat16
    )
    hidden_rows = hidden.reshape(-1, feature_width)
    hidden_sum = jnp.dot(
        hidden_rows,
        lax.all_gather(proj_in, "dp", axis=0, tiled=True),
        preferred_element_type=jnp.float32,
    )
    hidden_proj = hidden_sum.astype(jnp.bfloat16).reshape(groups, local_count, capacity, k_in)
    slot_shape = (groups, local_count, capacity)
    width = local_count * capacity
    all_grad, all_gate, all_routes, all_seq = (
        lax.all_gather(grad_proj, "expert", axis=0, tiled=True),
        lax.all_gather(gate_weights, "expert", axis=0, tiled=True),
        lax.all_gather(routes, "expert", axis=0, tiled=True),
        lax.all_gather(seq_ids, "expert", axis=0, tiled=True),
    )
    all_grad = all_grad.reshape(groups, token_count, k_out)
    all_gate = all_gate.reshape(groups, token_count, -1)
    all_routes = all_routes.reshape(groups, token_count, -1)
    start = lax.axis_index("expert") * width

    def tables(items):
        return slot_rows(items[0], items[1], items[2], items[3], start, width, capacity)

    grad_slots, slot_gate, slot_seq = lax.map(tables, (all_routes, all_gate, all_seq, all_grad))
    grad_slots = grad_slots.reshape(slot_shape + (k_out,))
    return sequence_totals(
        grad_slots, hidden_proj, slot_gate.reshape(slot_shape), slot_seq.reshape(slot_shape)
    )


def solution(mesh):
    placed = (
        P(("dp", "expert"), None),
        P(("dp", "expert"), None),
        P(("dp", "expert"), None),
        P(("dp", "expert"), None),
        P("dp", "expert", None, None),
        P("expert", None),
        P("dp", None),
    )
    return jax.shard_map(
        shards, mesh=mesh, in_specs=placed, out_specs=P("dp", "expert", None), check_vma=False
    )
```

profile of v0, /device:TPU:0, one launch (start us, length us, event | category | flops | bytes accessed | tf_op | source)
XLA Modules:
  0.0 172.9 jit_solution(12468886280944823600)
XLA Ops:
  6.5 0.7 all-gather.3.cloned.1.call-update
  7.3 28.1 %all_gather.22 = bf16[1024,8]{0,1:T(8,128)(2,1)S(1)} all-gather(bf16[128,8]{0,1:T(8,128)(2,1)} %param.10), channel_id=1, replica_groups=mesh['dp'=4,'expert'=8] {'expert'}, dimensions={0}, use_global_device_ids=true | all-gather | bytes 18432 | tf_op jit(solution)/shard_map/all_gather | solution.py:72
  35.6 30.8 %all_gather.19 = s32[1024,8]{0,1:T(8,128)S(1)} all-gather(s32[128,8]{0,1:T(8,128)} %param.11), channel_id=1, replica_groups=mesh['dp'=4,'expert'=8] {'expert'}, dimensions={0}, use_global_device_ids=true | all-gather | bytes 36864 | tf_op jit(solution)/shard_map/all_gather | solution.py:73
  66.6 5.6 %all_gather.18 = bf16[2048,32]{0,1:T(8,128)(2,1)S(1)} all-gather(bf16[512,32]{0,1:T(8,128)(2,1)} %param.15), channel_id=1, replica_groups=mesh['dp'=4,'expert'=8] {'dp'}, dimensions={0}, use_global_device_ids=true | all-gather | bytes 163840 | tf_op jit(solution)/shard_map/all_gather | solution.py:64
  72.2 4.8 %fusion.9 = f32[1536,32]{0,1:T(8,128)S(1)} fusion(bf16[1536,2048]{1,0:T(8,128)(2,1)} %bitcast.46, bf16[2048,32]{0,1:T(8,128)(2,1)S(1)} %all_gather.18), kind=kOutput, calls=%fused_computation.22 | convolution fusion | flops 201424896 | bytes 6619136 | tf_op jit(solution)/shard_map/dot_general | solution.py:62
  77.0 1.2 copy.24
  78.1 18.9 %all-gather = s32[8,1,128]{2,1,0:T(1,128)S(1)} all-gather(s32[1,1,128]{2,1,0:T(1,128)S(1)} %bitcast.53), channel_id=1, replica_groups=mesh['dp'=4,'expert'=8] {'expert'}, dimensions={0}, use_global_device_ids=true | all-gather | bytes 4608 | tf_op jit(solution)/shard_map/all_gather | solution.py:74
  97.1 2.1 %convolution_convert_fusion.2 = bf16[128,128]{1,0:T(8,128)(2,1)S(1)} fusion(bf16[128,7168]{1,0:T(8,128)(2,1)S(1)} %copy-done, bf16[7168,128]{1,0:T(8,128)(2,1)} %all-gather.3.cloned.1.call-done), kind=kOutput, calls=%fused_computation.27 | convolution fusion | flops 234897408 | bytes 3702784 | tf_op jit(solution)/shard_map/dot_general | solution.py:58
  99.2 30.7 %all_gather.21 = bf16[1024,128]{1,0:T(8,128)(2,1)S(1)} all-gather(bf16[128,128]{1,0:T(8,128)(2,1)S(1)} %convolution_convert_fusion.2), channel_id=1, replica_groups=mesh['dp'=4,'expert'=8] {'expert'}, dimensions={0}, use_global_device_ids=true | all-gather | bytes 294912 | tf_op jit(solution)/shard_map/all_gather | solution.py:71
  129.9 22.5 %while.14 = (s32[]{:T(128)}, bf16[8,192,128]{2,1,0:T(8,128)(2,1)}, bf16[8,192]{1,0:T(8,128)(2,1)S(1)}, s32[8,192]{1,0:T(8,128)S(1)}, s32[8,128,8]{2,1,0:T(8,128)...) while((s32[]{:T(128)}, bf16[8,192,128]{2,1,0:T(8,128)(2,1)}, ...), condition=%wide.region_5.6_spmd, body=%wide.region_0.5_spmd.sunk | while | flops 13111106 | bytes 253713 | solution.py:84
  130.4 0.5 convert_reduce_fusion.2
  132.0 0.8 fusion.34
  133.2 0.5 convert_reduce_fusion.2
  134.8 0.8 fusion.34
  136.0 0.5 convert_reduce_fusion.2
  137.6 0.8 fusion.34
  140.4 0.8 fusion.34
  143.2 0.8 fusion.34
  146.0 0.8 fusion.34
  148.9 0.8 fusion.34
  151.7 0.8 fusion.34
  152.6 3.5 %fusion.15 = bf16[8,2,8,128,32]{3,4,1,2,0:T(8,128)(2,1)S(1)} fusion(bf16[8,8,24,128,1]{3,2,4,1,0:T(8,128)(2,1)} %bitcast.54, f32[8,8,24,2]{2,3,1,0:T(2,128)S(1)} %compare_select_fusion.2, f32[8,8,24,32]{3,2,1,0:T(8,128)} %bitcast.48), kind=kOutput, calls=%fused_computation.26 | convolution fusion | flops 151617536 | bytes 1650688 | tf_op jit(solution)/shard_map/becs,beco,beci->bseoi/dot_general | solution.py:38
  156.2 3.1 %copy.22 = bf16[8,2,8,128,32]{4,3,2,1,0:T(8,128)(2,1)} copy(bf16[8,2,8,128,32]{3,4,1,2,0:T(8,128)(2,1)S(1)} %fusion.15) | data formatting | bytes 2097152 | tf_op jit(solution)/shard_map/convert_element_type | solution.py:46
  159.3 6.7 %convert_element_type.64 = bf16[16,8,4096]{2,1,0:T(8,128)(2,1)} reshape(bf16[8,2,8,128,32]{4,3,2,1,0:T(8,128)(2,1)} %copy.22) | data formatting | bytes 2097152 | tf_op jit(solution)/shard_map/convert_element_type | solution.py:46
  (163 shorter events, 14.8 us)
Async XLA Ops:
  6.5 90.5 %copy-start = (bf16[128,7168]{1,0:T(8,128)(2,1)S(1)}, bf16[128,7168]{1,0:T(8,128)(2,1)}, u32[]{:S(2)}) copy-start(bf16[128,7168]{1,0:T(8,128)(2,1)} %param.9) | copy-start | bytes 5505028
  6.5 90.5 %all-gather.3.cloned.1.call-start = ((), (), s32[]{:S(2)}) async-start(), calls=%async_computation | async-start | bytes 2064384 | tf_op jit(solution)/shard_map/all_gather | solution.py:57
  72.2 5.9 %copy-start.1 = (s32[1,128]{1,0:T(1,128)S(1)}, s32[1,128]{1,0:T(1,128)}, u32[]{:S(2)}) copy-start(s32[1,128]{1,0:T(1,128)} %param.12) | copy-start | bytes 1540
Sparse Core Ops, SparseCore 0:
  9.5 49.2 all-gather.2
where the time goes:
time: 173 us
  blocking collectives  114 us (66%)
  matrix products  16.5 us (10%)
  local copies, waits for them, and re-layouts  16.2 us (9%)
  between operations  13.5 us (8%)
  other arithmetic  11.2 us (6%)
    all_gather x1, blocking collectives, shards(): lax.all_gather(routes, 'expert', axis=0, tiled=True)  30.8 us
    all_gather x1, blocking collectives, shards(): lax.all_gather(grad_proj, 'expert', axis=0, tiled=True)  30.7 us
    all_gather x1, blocking collectives, shards(): lax.all_gather(gate_weights, 'expert', axis=0, tiled=True)  28.1 us
    all_gather x1, blocking collectives, shards(): lax.all_gather(seq_ids, 'expert', axis=0, tiled=True)  18.9 us
    convert_element_type x2, local copies, waits for them, and re-layouts, sequence_totals(): totals.reshape(groups * seq_count, local_count, k_out * k_in)  9.86 us
    dot_general x8, matrix products, slot_rows(): jnp.dot(token_pick, grad_block, preferred_element_type=jnp.float32)  6.13 us
    all_gather x1, blocking collectives, shards(): lax.all_gather(proj_in, 'dp', axis=0, tiled=True)  5.64 us
    dot_general x1, matrix products, shards(): jnp.dot(hidden_rows, lax.all_gather(proj_in, 'dp', axis=0, tiled=True), p...  4.75 us
  transfers between devices with their start and end apart: 1, of which 0 were waited for; matrix products, arithmetic and copies ran while one was open for 4% of the time, Pallas kernels for 0%

commit v1 on v0

v1 whole, which is shorter than its diff:
```python
import functools

import jax
import jax.numpy as jnp
from jax import lax
from jax.experimental import pallas as pl
from jax.experimental.pallas import tpu as pltpu
from jax.sharding import PartitionSpec as P

SEQ_DEV = 2
LANES = 128
MESH = pl.DeviceIdType.MESH
F32 = jnp.float32
BF16 = jnp.bfloat16


def iota(shape, dim):
    return lax.broadcasted_iota(jnp.int32, shape, dim)


def dot(a, b):
    return jnp.dot(a, b, preferred_element_type=F32)


def dot_nt(a, b):
    return lax.dot_general(a, b, (((1,), (1,)), ((), ())), preferred_element_type=F32)


def kernel(
    nd, ne, cap,
    og_hbm, gate_hbm, routes_hbm, seq_hbm, hid_hbm, po_hbm, pi_hbm, out_hbm,
    og, gate, routes, seq, hid, pall, pin, pin_all, pin4, tbl_mine, tbl_all, g_all,
    hp, pick, bd, stage, outv,
    og_sem, small_sem, hid_sem, po_sem, ring_send, ring_recv, sib_send, sib_recv,
    pin_send, pin_recv, tbl_send, tbl_recv, g_send, g_recv, out_sem,
):
    tokens = og.shape[0]
    shard = po_hbm.shape[0]
    k_out = po_hbm.shape[1]
    k_in = pi_hbm.shape[1]
    top = routes.shape[1]
    rows = hp.shape[1]
    local = rows // cap
    experts = ne * local
    quads = LANES // k_in
    groups = k_out // quads
    half = shard // 2
    cut = half // 32 * 16
    parts = ((0, cut), (cut, half - cut))
    far = ne // 2

    dp = lax.axis_index("dp")
    me = lax.axis_index("expert")
    core = lax.rem(dp, 2)
    sibling = dp + 1 - 2 * core
    odd = lax.rem(me, 2)
    here = (1 - odd) * (me // 2) + odd * (ne - 1 - me // 2)

    def at(place):
        place = lax.rem(place + 2 * ne, ne)
        back = place // (ne // 2)
        return (1 - back) * (2 * place) + back * (2 * (ne - 1 - place) + 1)

    small = [
        pltpu.make_async_copy(pi_hbm, pin, small_sem.at[0]),
        pltpu.make_async_copy(routes_hbm, routes, small_sem.at[1]),
        pltpu.make_async_copy(gate_hbm, gate, small_sem.at[2]),
        pltpu.make_async_copy(seq_hbm, seq, small_sem.at[3]),
    ]
    own_rows = pl.ds(pl.multiple_of(me * shard, 16), shard)
    own = pltpu.make_async_copy(po_hbm, pall.at[own_rows, :], po_sem)
    grads = pltpu.make_async_copy(og_hbm, og, og_sem)
    for copy in small:
        copy.start()
    own.start()
    grads.start()

    def hidden_copy(b):
        return pltpu.make_async_copy(
            hid_hbm.at[pl.ds(b * rows, rows), :], hid.at[b], hid_sem.at[b]
        )

    for b in range(ne):
        hidden_copy(b).start()

    barrier = pltpu.get_barrier_semaphore()
    for k in range(1, ne):
        pl.semaphore_signal(
            barrier, inc=1, device_id=(dp, lax.rem(me + k, ne)), device_id_type=MESH
        )
    for k in range(1, nd):
        pl.semaphore_signal(
            barrier, inc=1, device_id=(lax.rem(dp + k, nd), me), device_id_type=MESH
        )
    pl.semaphore_wait(barrier, ne + nd - 2)

    def step(way):
        return 1 - 2 * way

    def uses(way, d):
        return (0, 1) if d < far else (way,)

    def span(source, part, side):
        first, size = parts[part]
        return pl.ds(pl.multiple_of(source * shard + side * half + first, 16), size)

    def ring(way, d, part):
        source = at(here - step(way) * (d - 1))
        first, size = parts[part]
        if d == 1:
            src = po_hbm.at[pl.ds(pl.multiple_of(core * half + first, 16), size), :]
        else:
            src = pall.at[span(source, part, core), :]
        return pltpu.make_async_remote_copy(
            src_ref=src,
            dst_ref=pall.at[span(source, part, core), :],
            send_sem=ring_send.at[way, d - 1, part],
            recv_sem=ring_recv.at[way, d - 1, part],
            device_id=(dp, at(here + step(way))),
            device_id_type=MESH,
        )

    def ring_arrival(way, d, part):
        source = at(here - step(way) * d)
        block = pall.at[span(source, part, core), :]
        return pltpu.make_async_remote_copy(
            src_ref=block,
            dst_ref=block,
            send_sem=ring_send.at[way, d - 1, part],
            recv_sem=ring_recv.at[way, d - 1, part],
            device_id=(dp, at(here + step(way))),
            device_id_type=MESH,
        )

    def hand_over(way, d, part, side):
        source = at(here - step(way) * d)
        block = pall.at[span(source, part, side), :]
        return pltpu.make_async_remote_copy(
            src_ref=block,
            dst_ref=block,
            send_sem=sib_send.at[way, d - 1, part],
            recv_sem=sib_recv.at[way, d - 1, part],
            device_id=(sibling, me),
            device_id_type=MESH,
        )

    def relay(d):
        for part in (0, 1):
            for way in (0, 1):
                if part in uses(way, d):
                    ring_arrival(way, d, part).wait_recv()
                    if d < far and part in uses(way, d + 1):
                        ring(way, d + 1, part).start()
                    hand_over(way, d, part, core).start()

    def handed(d):
        for way in (0, 1):
            for part in uses(way, d):
                hand_over(way, d, part, 1 - core).wait_recv()

    for part in (0, 1):
        for way in (0, 1):
            ring(way, 1, part).start()

    def pin_copy(k):
        return pltpu.make_async_remote_copy(
            src_ref=pin_all.at[dp],
            dst_ref=pin_all.at[dp],
            send_sem=pin_send.at[k - 1],
            recv_sem=pin_recv.at[k - 1],
            device_id=(lax.rem(dp + k, nd), me),
            device_id_type=MESH,
        )

    def pin_arrival(k):
        block = pin_all.at[lax.rem(dp + nd - k, nd)]
        return pltpu.make_async_remote_copy(
            src_ref=block,
            dst_ref=block,
            send_sem=pin_send.at[k - 1],
            recv_sem=pin_recv.at[k - 1],
            device_id=(lax.rem(dp + k, nd), me),
            device_id_type=MESH,
        )

    small[0].wait()
    eye = (iota((k_in, k_in), 0) == iota((k_in, k_in), 1)).astype(F32).astype(BF16)
    pin_all[dp] = dot_nt(eye, pin[...]).astype(BF16)
    for k in range(1, nd):
        pin_copy(k).start()

    def exchange(buffer, sends, receives, k, mine):
        if mine:
            src, dst = buffer
        else:
            dst = buffer[1]
            src = dst
        return pltpu.make_async_remote_copy(
            src_ref=src,
            dst_ref=dst,
            send_sem=sends.at[k - 1],
            recv_sem=receives.at[k - 1],
            device_id=(dp, lax.rem(me + k, ne)),
            device_id_type=MESH,
        )

    def table_copy(k):
        return exchange(
            (tbl_mine.at[lax.rem(me + k, ne)], tbl_all.at[me]), tbl_send, tbl_recv, k, True
        )

    def table_arrival(k):
        return exchange(
            (None, tbl_all.at[lax.rem(me + ne - k, ne)]), tbl_send, tbl_recv, k, False
        )

    for copy in small[1:]:
        copy.wait()
    eye_top = (iota((top, top), 0) == iota((top, top), 1)).astype(F32).astype(BF16)
    routes_t = dot_nt(eye_top, routes[...].astype(F32).astype(BF16))
    gates_t = dot_nt(eye_top, gate[...])
    number = iota((experts, tokens), 0)
    number_f = number.astype(F32)
    named = jnp.zeros((experts, tokens), F32)
    weight = jnp.zeros((experts, tokens), F32)
    for k in range(top):
        same = number_f == routes_t[k : k + 1, :]
        named = jnp.where(same, 1.0, named)
        weight = jnp.where(same, gates_t[k : k + 1, :], weight)
    earlier = (iota((tokens, tokens), 0) < iota((tokens, tokens), 1)).astype(F32).astype(BF16)
    slots = dot(named.astype(BF16), earlier)
    base = (lax.rem(number, local) * cap).astype(F32)
    code = jnp.where(named > 0.0, slots + base, -1.0)
    seq_row = seq[...]
    for k in range(ne):
        pick_rows = slice(k * local, (k + 1) * local)
        tbl_mine[k, 0:local, :] = code[pick_rows]
        for s in range(SEQ_DEV):
            tbl_mine[k, (s + 1) * local : (s + 2) * local, :] = jnp.where(
                seq_row == s, weight[pick_rows], 0.0
            )
    for k in range(1, ne):
        table_copy(k).start()
    tbl_all[me] = tbl_mine[me]

    relay(1)

    for k in range(1, nd):
        pin_arrival(k).wait_recv()
    width = pin_all.shape[2]
    for d in range(nd):
        for q in range(quads):
            pin4[q * k_in : (q + 1) * k_in, d * width : (d + 1) * width] = pin_all[d]

    def project(first, last):
        def one(b, carry):
            hidden_copy(b).wait()
            hp[b] = dot_nt(hid[b], pin4[...]).astype(BF16)
            return carry

        lax.fori_loop(first, last, one, 0)

    project(0, ne // 2)
    relay(2)
    project(ne // 2, ne)
    for k in range(1, ne):
        table_arrival(k).wait_recv()
    if far > 2:
        relay(3)

    row = iota((rows, local), 0)
    col = iota((rows, local), 1) * cap
    spread = ((row >= col) & (row < col + cap)).astype(F32).astype(BF16)
    ones = jnp.ones((tokens, LANES), BF16)
    row_f = iota((rows, tokens), 0).astype(F32)
    row_l = iota((rows, LANES), 0)

    def weigh(b, carry):
        placed = dot(spread, tbl_all[b, 0:local, :].astype(BF16)) == row_f
        pick[b] = jnp.where(placed, 1.0, 0.0).astype(BF16)
        stored = hp[b].astype(F32)
        for s in range(SEQ_DEV):
            gates = dot(spread, tbl_all[b, (s + 1) * local : (s + 2) * local, :].astype(BF16))
            amount = dot(jnp.where(placed, gates, 0.0).astype(BF16), ones)
            scaled = stored * amount
            for e in range(local):
                mine = (row_l >= e * cap) & (row_l < (e + 1) * cap)
                first = (s * local + e) * LANES
                bd[b, :, first : first + LANES] = jnp.where(mine, scaled, 0.0).astype(BF16)
        return carry

    own.wait()
    grads.wait()
    aligned = shard % LANES == 0

    def product(source):
        columns = pl.ds(pl.multiple_of(source * shard, LANES), shard)
        block = pl.ds(pl.multiple_of(source * shard, 16), shard)
        return dot(og[:, columns], pall[block, :])

    total = jnp.zeros((tokens, k_out), F32)
    if aligned:
        total = total + product(me)

    def add(total, d):
        handed(d)
        if aligned:
            total = total + product(at(here + d))
            if d < far:
                total = total + product(at(here - d))
        return total

    total = add(total, 1)
    lax.fori_loop(0, ne, weigh, 0)
    for d in range(4, far + 1):
        relay(d)
    for d in range(2, far + 1):
        total = add(total, d)
    if not aligned:
        total = dot(og[...], pall[...])

    r = iota((k_out, k_out), 0)
    wanted = quads * lax.rem(r, groups) + lax.div(r, groups)
    shuffle = (wanted == iota((k_out, k_out), 1)).astype(F32).astype(BF16)
    g_all[me] = dot_nt(shuffle, total.astype(BF16)).astype(BF16)

    def grad_copy(k):
        return exchange((g_all.at[me], g_all.at[me]), g_send, g_recv, k, True)

    def grad_arrival(k):
        return exchange(
            (None, g_all.at[lax.rem(me + ne - k, ne)]), g_send, g_recv, k, False
        )

    for k in range(1, ne):
        grad_copy(k).start()

    quad = lax.div(lax.rem(iota((groups, 2 * LANES), 1), LANES), k_in)

    def out_copy(b):
        return pltpu.make_async_copy(
            outv.at[pl.ds(SEQ_DEV * b, SEQ_DEV)],
            out_hbm.at[pl.ds(SEQ_DEV * b, SEQ_DEV)],
            out_sem.at[b],
        )

    for k in range(ne):
        b = lax.rem(me + ne - k, ne)
        if k:
            grad_arrival(k).wait_recv()
        chosen = dot_nt(g_all[b], pick[b]).astype(BF16)
        for s in range(SEQ_DEV):
            for e in range(0, local, 2):
                first = (s * local + e) * LANES
                full = dot(chosen, bd[b, :, first : first + 2 * LANES])
                value = full[0:groups]
                for q in range(1, quads):
                    value = jnp.where(quad == q, full[q * groups : (q + 1) * groups], value)
                place = s * groups * local + e
                stage[pl.ds(place, groups, stride=local), :] = value[:, :LANES]
                stage[pl.ds(place + 1, groups, stride=local), :] = value[:, LANES:]
            for j in range(groups):
                place = (s * groups + j) * local
                outv[SEQ_DEV * b + s, :, j * LANES : (j + 1) * LANES] = stage[
                    place : place + local, :
                ].astype(BF16)
        out_copy(b).start()

    for k in range(1, ne):
        grad_copy(k).wait_send()
        table_copy(k).wait_send()
    for k in range(1, nd):
        pin_copy(k).wait_send()
    for d in range(1, far + 1):
        for way in (0, 1):
            for part in uses(way, d):
                ring(way, d, part).wait_send()
                hand_over(way, d, part, core).wait_send()
    for b in range(ne):
        out_copy(b).wait()


def shards(nd, ne, out_grad, gate_weights, routes, seq_ids, hidden, proj_out, proj_in):
    blocks, local, cap, width = hidden.shape
    tokens, features = out_grad.shape
    k_out, k_in = proj_out.shape[1], proj_in.shape[1]
    rows = local * cap
    far = ne // 2
    dma = pltpu.SemaphoreType.DMA
    return pl.pallas_call(
        functools.partial(kernel, nd, ne, cap),
        out_shape=jax.ShapeDtypeStruct((blocks * SEQ_DEV, local, k_out * k_in), BF16),
        in_specs=[pl.BlockSpec(memory_space=pl.ANY)] * 7,
        out_specs=pl.BlockSpec(memory_space=pl.ANY),
        scratch_shapes=[
            pltpu.VMEM((tokens, features), BF16),
            pltpu.VMEM(gate_weights.shape, BF16),
            pltpu.VMEM(routes.shape, jnp.int32),
            pltpu.VMEM(seq_ids.shape, jnp.int32),
            pltpu.VMEM((blocks, rows, width), BF16),
            pltpu.VMEM((features, k_out), BF16),
            pltpu.VMEM(proj_in.shape, BF16),
            pltpu.VMEM((nd, k_in, width // nd), BF16),
            pltpu.VMEM((LANES, width), BF16),
            pltpu.VMEM((ne, (SEQ_DEV + 1) * local, tokens), F32),
            pltpu.VMEM((ne, (SEQ_DEV + 1) * local, tokens), F32),
            pltpu.VMEM((ne, k_out, tokens), BF16),
            pltpu.VMEM((ne, rows, LANES), BF16),
            pltpu.VMEM((ne, rows, tokens), BF16),
            pltpu.VMEM((ne, rows, SEQ_DEV * local * LANES), BF16),
            pltpu.VMEM((SEQ_DEV * local * k_out * k_in // LANES, LANES), F32),
            pltpu.VMEM((blocks * SEQ_DEV, local, k_out * k_in), BF16),
            dma, dma((4,)), dma((ne,)), dma,
            dma((2, far, 2)), dma((2, far, 2)), dma((2, far, 2)), dma((2, far, 2)),
            dma((nd - 1,)), dma((nd - 1,)), dma((ne - 1,)), dma((ne - 1,)),
            dma((ne - 1,)), dma((ne - 1,)), dma((ne,)),
        ],
        compiler_params=pltpu.CompilerParams(
            collective_id=0, has_side_effects=True, vmem_limit_bytes=48 * 1024 * 1024
        ),
    )(out_grad, gate_weights, routes, seq_ids, hidden.reshape(-1, width), proj_out, proj_in)


def solution(mesh):
    placed = (
        P(("dp", "expert"), None),
        P(("dp", "expert"), None),
        P(("dp", "expert"), None),
        P(("dp", "expert"), None),
        P("dp", "expert", None, None),
        P("expert", None),
        P("dp", None),
    )
    return jax.shard_map(
        functools.partial(shards, mesh.shape["dp"], mesh.shape["expert"]),
        mesh=mesh,
        in_specs=placed,
        out_specs=P("dp", "expert", None),
        check_vma=False,
    )
```

time: 173 us -> 41.1 us (0.24)
  blocking collectives: 114 us -> 0 us
  Pallas kernels: 0 us -> 34.2 us
  matrix products: 16.5 us -> 0 us
  between operations: 13.5 us -> 0.02 us
  other arithmetic: 11.2 us -> 0 us
  local copies, waits for them, and re-layouts: 16.2 us -> 6.53 us
    all_gather x5 -> x0, blocking collectives: 114 us -> none  [the longest x1 30.8 us: shards(): lax.all_gather(routes, 'expert', axis=0, tiled=True)]
    pallas_call x0 -> x1, Pallas kernels: none -> 34.2 us  [shards(): pl.pallas_call(functools.partial(kernel, nd, ne, cap), out_shape=jax.Shap...]
    dot_general x11 -> x0, matrix products: 16.5 us -> none  [the longest x8 6.13 us: slot_rows(): jnp.dot(token_pick, grad_block, preferred_element_type=jnp.float32)]
    convert_element_type x19 -> x0, local copies, waits for them, and re-layouts: 10.7 us -> none  [the longest x2 9.86 us: sequence_totals(): totals.reshape(groups * seq_count, local_count, k_out * k_in)]
    reduce_sum x24 -> x0, other arithmetic: 7.86 us -> none  [the longest x8 4.2 us: slot_rows(): ranks = jnp.sum((same & before).astype(jnp.int32), axis=1)]
    unnamed x4 -> x10, local copies, waits for them, and re-layouts: 0.01 us -> 6.53 us
    reduce_or x8 -> x0, other arithmetic: 2.99 us -> none  [slot_rows(): jnp.any(select.reshape(slot_count, token_count, choice_count), axis=2)]
  transfers between devices with their start and end apart: 1 -> 0, of which waited for: 0 -> 0; matrix products, arithmetic and copies ran while one was open for 4% -> 0% of each run, Pallas kernels for 0% -> 0%
where the time goes in v1:
time: 41.1 us; the launch traced here: 40.8 us
  Pallas kernels  34.2 us (83%)
  local copies, waits for them, and re-layouts  6.53 us (16%)
    pallas_call x1, Pallas kernels, shards(): pl.pallas_call(functools.partial(kernel, nd, ne, cap), out_shape=jax.Shap...  34.2 us
    unnamed x10, local copies, waits for them, and re-layouts  6.53 us

profile of v1, /device:TPU:0, one launch (start us, length us, event | category | flops | bytes accessed | tf_op | source)
XLA Modules:
  0.0 40.8 jit_solution(16697340369296906625)
XLA Ops:
  0.0 0.8 %copy.8.gate_hbm = bf16[128,8]{1,0:T(8,128)(2,1)S(1)} copy(bf16[128,8]{0,1:T(8,128)(2,1)} %param.8) | data formatting | bytes 4096 | tf_op args[1]
  0.8 0.8 %copy.9.routes_hbm = s32[128,8]{1,0:T(8,128)S(1)} copy(s32[128,8]{0,1:T(8,128)} %param.9) | data formatting | bytes 8192 | tf_op args[2]
  1.6 0.9 %copy.10.pi_hbm = bf16[512,32]{1,0:T(8,128)(2,1)S(1)} copy(bf16[512,32]{0,1:T(8,128)(2,1)} %param.13) | data formatting | bytes 65536 | tf_op args[6]
  2.5 0.0 copy-start
  2.5 1.5 %copy-done = bf16[128,7168]{1,0:T(8,128)(2,1)S(1)} copy-done((bf16[128,7168]{1,0:T(8,128)(2,1)S(1)}, bf16[128,7168]{1,0:T(8,128)(2,1)}, u32[]{:S(2)}) %copy-start) | copy-done | bytes 1835032
  4.0 0.0 copy-start.1
  4.0 0.9 %copy-done.1 = bf16[896,128]{1,0:T(8,128)(2,1)S(1)} copy-done((bf16[896,128]{1,0:T(8,128)(2,1)S(1)}, bf16[896,128]{1,0:T(8,128)(2,1)}, u32[]{:S(2)}) %copy-start.1) | copy-done | bytes 229400
  4.9 0.0 copy-start.2
  4.9 0.7 %copy-done.2 = s32[1,128]{1,0:T(1,128)S(1)} copy-done((s32[1,128]{1,0:T(1,128)S(1)}, s32[1,128]{1,0:T(1,128)}, u32[]{:S(2)}) %copy-start.2) | copy-done | bytes 536
  5.6 34.2 %shard_map.73 = bf16[16,8,4096]{2,1,0:T(8,128)(2,1)S(1)} custom-call(bf16[128,7168]{1,0:T(8,128)(2,1)S(1)} %copy-done, bf16[128,8]{1,0:T(8,128)(2,1)S(1)} %copy.8.gate_hbm, s32[128,8]{1,0:T(8,128)S(1)} %copy.9.routes_hbm, s32[1,128]{1,0:T(1,128)S(1)} %copy-done.2, bf16[1536,2048]{1,0:T(8,128)(2,1)} %bitcast.1, bf16[896,128]{1,0:T(8,128)(2,1)S(1)} %copy-done.1, ...), custom_call_target="tpu_custom_call" | custom-call | tf_op jit(solution)/shard_map/pallas_call | solution.py:390
  39.8 1.0 %copy.12 = bf16[16,8,4096]{2,1,0:T(8,128)(2,1)} copy(bf16[16,8,4096]{2,1,0:T(8,128)(2,1)S(1)} %shard_map.73) | data formatting | bytes 2097152
Async XLA Ops:
  2.5 1.5 %copy-start = (bf16[128,7168]{1,0:T(8,128)(2,1)S(1)}, bf16[128,7168]{1,0:T(8,128)(2,1)}, u32[]{:S(2)}) copy-start(bf16[128,7168]{1,0:T(8,128)(2,1)} %og_hbm.1) | copy-start | bytes 5505028
  4.0 0.9 %copy-start.1 = (bf16[896,128]{1,0:T(8,128)(2,1)S(1)}, bf16[896,128]{1,0:T(8,128)(2,1)}, u32[]{:S(2)}) copy-start(bf16[896,128]{1,0:T(8,128)(2,1)} %po_hbm.1) | copy-start | bytes 688132
  4.9 0.7 %copy-start.2 = (s32[1,128]{1,0:T(1,128)S(1)}, s32[1,128]{1,0:T(1,128)}, u32[]{:S(2)}) copy-start(s32[1,128]{1,0:T(1,128)} %seq_hbm.1) | copy-start | bytes 1540

commit v2 on v1

--- a/solution.py
+++ b/solution.py
@@ -28,17 +28,17 @@
 
 def kernel(
     nd, ne, cap,
-    og_hbm, gate_hbm, routes_hbm, seq_hbm, hid_hbm, po_hbm, pi_hbm, out_hbm,
-    og, gate, routes, seq, hid, pall, pin, pin_all, pin4, tbl_mine, tbl_all, g_all,
-    hp, pick, bd, stage, outv,
+    og_hbm, gate_hbm, routes_hbm, seq_hbm, hid_hbm, po_hbm, pi_hbm, outv,
+    og, gate, routes, seq, hid, pall, pin_all, pin4, tbl_mine, tbl_all, g_all,
+    hp, pick, bd, stage,
     og_sem, small_sem, hid_sem, po_sem, ring_send, ring_recv, sib_send, sib_recv,
-    pin_send, pin_recv, tbl_send, tbl_recv, g_send, g_recv, out_sem,
+    pin_send, pin_recv, tbl_send, tbl_recv, g_send, g_recv,
 ):
     tokens = og.shape[0]
     shard = po_hbm.shape[0]
     k_out = po_hbm.shape[1]
-    k_in = pi_hbm.shape[1]
-    top = routes.shape[1]
+    k_in = pi_hbm.shape[0]
+    top = routes.shape[0]
     rows = hp.shape[1]
     local = rows // cap
     experts = ne * local
@@ -62,7 +62,7 @@
         return (1 - back) * (2 * place) + back * (2 * (ne - 1 - place) + 1)
 
     small = [
-        pltpu.make_async_copy(pi_hbm, pin, small_sem.at[0]),
+        pltpu.make_async_copy(pi_hbm, pin_all.at[dp], small_sem.at[0]),
         pltpu.make_async_copy(routes_hbm, routes, small_sem.at[1]),
         pltpu.make_async_copy(gate_hbm, gate, small_sem.at[2]),
         pltpu.make_async_copy(seq_hbm, seq, small_sem.at[3]),
@@ -184,8 +184,6 @@
         )
 
     small[0].wait()
-    eye = (iota((k_in, k_in), 0) == iota((k_in, k_in), 1)).astype(F32).astype(BF16)
-    pin_all[dp] = dot_nt(eye, pin[...]).astype(BF16)
     for k in range(1, nd):
         pin_copy(k).start()
 
@@ -216,15 +214,13 @@
 
     for copy in small[1:]:
         copy.wait()
-    eye_top = (iota((top, top), 0) == iota((top, top), 1)).astype(F32).astype(BF16)
-    routes_t = dot_nt(eye_top, routes[...].astype(F32).astype(BF16))
-    gates_t = dot_nt(eye_top, gate[...])
+    routes_t = routes[...]
+    gates_t = gate[...].astype(F32)
     number = iota((experts, tokens), 0)
-    number_f = number.astype(F32)
     named = jnp.zeros((experts, tokens), F32)
     weight = jnp.zeros((experts, tokens), F32)
     for k in range(top):
-        same = number_f == routes_t[k : k + 1, :]
+        same = number == routes_t[k : k + 1, :]
         named = jnp.where(same, 1.0, named)
         weight = jnp.where(same, gates_t[k : k + 1, :], weight)
     earlier = (iota((tokens, tokens), 0) < iota((tokens, tokens), 1)).astype(F32).astype(BF16)
@@ -336,13 +332,6 @@
         grad_copy(k).start()
 
     quad = lax.div(lax.rem(iota((groups, 2 * LANES), 1), LANES), k_in)
-
-    def out_copy(b):
-        return pltpu.make_async_copy(
-            outv.at[pl.ds(SEQ_DEV * b, SEQ_DEV)],
-            out_hbm.at[pl.ds(SEQ_DEV * b, SEQ_DEV)],
-            out_sem.at[b],
-        )
 
     for k in range(ne):
         b = lax.rem(me + ne - k, ne)
@@ -364,7 +353,6 @@
                 outv[SEQ_DEV * b + s, :, j * LANES : (j + 1) * LANES] = stage[
                     place : place + local, :
                 ].astype(BF16)
-        out_copy(b).start()
 
     for k in range(1, ne):
         grad_copy(k).wait_send()
@@ -376,8 +364,6 @@
             for part in uses(way, d):
                 ring(way, d, part).wait_send()
                 hand_over(way, d, part, core).wait_send()
-    for b in range(ne):
-        out_copy(b).wait()
 
 
 def shards(nd, ne, out_grad, gate_weights, routes, seq_ids, hidden, proj_out, proj_in):
@@ -390,16 +376,15 @@
     return pl.pallas_call(
         functools.partial(kernel, nd, ne, cap),
         out_shape=jax.ShapeDtypeStruct((blocks * SEQ_DEV, local, k_out * k_in), BF16),
-        in_specs=[pl.BlockSpec(memory_space=pl.ANY)] * 7,
-        out_specs=pl.BlockSpec(memory_space=pl.ANY),
+        in_specs=[pl.BlockSpec(memory_space=pltpu.HBM)] * 7,
+        out_specs=pl.BlockSpec(memory_space=pltpu.VMEM),
         scratch_shapes=[
             pltpu.VMEM((tokens, features), BF16),
-            pltpu.VMEM(gate_weights.shape, BF16),
-            pltpu.VMEM(routes.shape, jnp.int32),
+            pltpu.VMEM(gate_weights.shape[::-1], BF16),
+            pltpu.VMEM(routes.shape[::-1], jnp.int32),
             pltpu.VMEM(seq_ids.shape, jnp.int32),
             pltpu.VMEM((blocks, rows, width), BF16),
             pltpu.VMEM((features, k_out), BF16),
-            pltpu.VMEM(proj_in.shape, BF16),
             pltpu.VMEM((nd, k_in, width // nd), BF16),
             pltpu.VMEM((LANES, width), BF16),
             pltpu.VMEM((ne, (SEQ_DEV + 1) * local, tokens), F32),
@@ -409,16 +394,17 @@
             pltpu.VMEM((ne, rows, tokens), BF16),
             pltpu.VMEM((ne, rows, SEQ_DEV * local * LANES), BF16),
             pltpu.VMEM((SEQ_DEV * local * k_out * k_in // LANES, LANES), F32),
-            pltpu.VMEM((blocks * SEQ_DEV, local, k_out * k_in), BF16),
             dma, dma((4,)), dma((ne,)), dma,
             dma((2, far, 2)), dma((2, far, 2)), dma((2, far, 2)), dma((2, far, 2)),
             dma((nd - 1,)), dma((nd - 1,)), dma((ne - 1,)), dma((ne - 1,)),
-            dma((ne - 1,)), dma((ne - 1,)), dma((ne,)),
+            dma((ne - 1,)), dma((ne - 1,)),
         ],
         compiler_params=pltpu.CompilerParams(
-            collective_id=0, has_side_effects=True, vmem_limit_bytes=48 * 1024 * 1024
+            collective_id=0, has_side_effects=True, vmem_limit_bytes=63 * 1024 * 1024 + 512 * 1024
         ),
-    )(out_grad, gate_weights, routes, seq_ids, hidden.reshape(-1, width), proj_out, proj_in)
+    )(
+        out_grad, gate_weights.T, routes.T, seq_ids, hidden.reshape(-1, width), proj_out, proj_in.T
+    )
 
 
 def solution(mesh):

time: 41.1 us -> 36.3 us (0.88)
  local copies, waits for them, and re-layouts: 6.53 us -> 2.29 us
    unnamed x10 -> x1, local copies, waits for them, and re-layouts: 6.53 us -> 2.29 us
where the time goes in v2:
time: 36.3 us; the launch traced here: 36.1 us
  Pallas kernels  33.8 us (93%)
  local copies, waits for them, and re-layouts  2.29 us (6%)
    pallas_call x1, Pallas kernels, shards(): pl.pallas_call(functools.partial(kernel, nd, ne, cap), out_shape=jax.Shap...  33.8 us
    unnamed x1, local copies, waits for them, and re-layouts  2.29 us

profile of v2, /device:TPU:0, one launch (start us, length us, event | category | flops | bytes accessed | tf_op | source)
XLA Modules:
  0.0 36.1 jit_solution(14380714262921920270)
XLA Ops:
  0.0 33.8 %shard_map.73 = bf16[16,8,4096]{2,1,0:T(8,128)(2,1)} custom-call(bf16[128,7168]{1,0:T(8,128)(2,1)} %og_hbm.1, bf16[8,128]{1,0:T(8,128)(2,1)} %bitcast.7, s32[8,128]{1,0:T(8,128)} %bitcast.6, s32[1,128]{1,0:T(1,128)} %seq_hbm.1, bf16[1536,2048]{1,0:T(8,128)(2,1)} %bitcast.4, bf16[896,128]{1,0:T(8,128)(2,1)} %po_hbm.1, bf16[32,512]{1,0:T(8,128)(2,1)} %bitcast.5), custom_call_target="tpu_custom_call" | custom-call | tf_op jit(solution)/shard_map/pallas_call | solution.py:376
  33.8 2.3 %copy.9 = bf16[16,8,4096]{2,1,0:T(8,128)(2,1)} copy(bf16[16,8,4096]{2,1,0:T(8,128)(2,1)} %shard_map.73) | data formatting | bytes 2097152

commit v3 on v2

--- a/solution.py
+++ b/solution.py
@@ -375,7 +375,7 @@
     dma = pltpu.SemaphoreType.DMA
     return pl.pallas_call(
         functools.partial(kernel, nd, ne, cap),
-        out_shape=jax.ShapeDtypeStruct((blocks * SEQ_DEV, local, k_out * k_in), BF16),
+        out_shape=pltpu.VMEM((blocks * SEQ_DEV, local, k_out * k_in), BF16),
         in_specs=[pl.BlockSpec(memory_space=pltpu.HBM)] * 7,
         out_specs=pl.BlockSpec(memory_space=pltpu.VMEM),
         scratch_shapes=[
@@ -400,7 +400,7 @@
             dma((ne - 1,)), dma((ne - 1,)),
         ],
         compiler_params=pltpu.CompilerParams(
-            collective_id=0, has_side_effects=True, vmem_limit_bytes=63 * 1024 * 1024 + 512 * 1024
+            collective_id=0, has_side_effects=True, vmem_limit_bytes=56 * 1024 * 1024
         ),
     )(
         out_grad, gate_weights.T, routes.T, seq_ids, hidden.reshape(-1, width), proj_out, proj_in.T

time: 36.3 us -> 34 us (0.937)
  local copies, waits for them, and re-layouts: 2.29 us -> 0.97 us
  Pallas kernels: 33.8 us -> 32.9 us
    unnamed x1, local copies, waits for them, and re-layouts: 2.29 us -> 0.97 us
    pallas_call x1, Pallas kernels: 33.8 us -> 32.9 us  [shards(): pl.pallas_call(functools.partial(kernel, nd, ne, cap), out_shape=pltpu.VM...]
where the time goes in v3:
time: 34 us; the launch traced here: 33.8 us
  Pallas kernels  32.9 us (97%)
  local copies, waits for them, and re-layouts  0.97 us (3%)
    pallas_call x1, Pallas kernels, shards(): pl.pallas_call(functools.partial(kernel, nd, ne, cap), out_shape=pltpu.VM...  32.9 us
    unnamed x1, local copies, waits for them, and re-layouts  0.97 us

profile of v3, /device:TPU:0, one launch (start us, length us, event | category | flops | bytes accessed | tf_op | source)
XLA Modules:
  0.0 33.8 jit_solution(12631416223443620257)
XLA Ops:
  0.0 32.9 %shard_map.73 = bf16[16,8,4096]{2,1,0:T(8,128)(2,1)S(1)} custom-call(bf16[128,7168]{1,0:T(8,128)(2,1)} %og_hbm.1, bf16[8,128]{1,0:T(8,128)(2,1)} %bitcast.7, s32[8,128]{1,0:T(8,128)} %bitcast.6, s32[1,128]{1,0:T(1,128)} %seq_hbm.1, bf16[1536,2048]{1,0:T(8,128)(2,1)} %bitcast.4, bf16[896,128]{1,0:T(8,128)(2,1)} %po_hbm.1, bf16[32,512]{1,0:T(8,128)(2,1)} %bitcast.5), custom_call_target="tpu_custom_call" | custom-call | tf_op jit(solution)/shard_map/pallas_call | solution.py:376
  32.9 1.0 %copy.9 = bf16[16,8,4096]{2,1,0:T(8,128)(2,1)} copy(bf16[16,8,4096]{2,1,0:T(8,128)(2,1)S(1)} %shard_map.73) | data formatting | bytes 2097152
